TPU v7x, 256 devices: a whole 4x4x8 slice. The times are simulated.
256 devices in a mesh: space: 128 (over y_hi, x, z, core), chan: 2 (over y_lo).
Axes of the slice: x: 4, y: 4 (y_hi: 2, y_lo: 2; y = y_hi * 2 + y_lo), z: 8, core: 2. Of those that a mesh axis runs over, the one named last changes fastest.
Arguments:
- features: bfloat16 [256, 16, 32, 256], P('space'), may hold values from -24 to 24
- kernel: bfloat16 [256, 27, 512], P(None, None, 'chan'), may hold values from -0.078125 to 0.078125
- cotangent: bfloat16 [256, 16, 32, 512], P('space', None, None, 'chan'), may hold values from -6 to 6
Outputs:
- input_grad: bfloat16 [256, 16, 32, 256], P('space', None, None, 'chan')
- kernel_grad: float32 [256, 27, 512], P('space', None, 'chan')
All inputs are finite; a program needn't handle non-finite values.
Results may differ from a plain program's by a relative error of at most 0.012.
Values may be sent and summed in bfloat16 or wider, within the bound.
A program may use at most 192 MiB of HBM per device.

v0:
```python
import jax
import jax.numpy as jnp
from jax import lax
from jax.experimental import pallas as pl
from jax.experimental.pallas import tpu as pltpu
from jax.sharding import PartitionSpec as P

BF = jnp.bfloat16
F32 = jnp.float32
MESH = pl.DeviceIdType.MESH

NY, NX, NZ = 2, 4, 8
SY, SZ, C = 16, 32, 256
CELLS = SY * SZ
HALO = CELLS + 2 * SZ
HALF = 128

Y_SET = (0, 1, 2, 3, 4)
X_SET = (5, 6, 7, 8)
ORDER = (0, 5, 1, 6, 2, 7, 3, 8, 4)

NT = (((1,), (1,)), ((), ()))


def block_rows(groups):
    return -(-6 * len(groups) // 16) * 16


BX, BY = block_rows(X_SET), block_rows(Y_SET)


def device(y, x, z, core):
    return ((y * NX + x) * NZ + z) * 2 + core


def spread(plane, sign, store):
    wide = plane.reshape(SY, SZ, C)
    wide32 = wide.astype(F32)
    for ci, c in enumerate((-1, 0, 1)):
        part = wide if c == 0 else pltpu.roll(wide32, (sign * c) % SZ, 1).astype(BF)
        store(ci, part.reshape(CELLS, C))


def fused(
    feat, kern, cot, ig_out, kg_out,
    kv, fb, ct, fs, pr, ps, ft, acc, pkx, pky,
    xr1, s1x, yr2, yr1, s1y, xr2, s2x, s2y, zsx, zsy, zrx, zry,
    own, igs, igr, permx, permy, sel,
    ig_sum, kg_sum,
    loc, f_s, f_r, g_s, g_r, x1_s, x1_r, y2_s, y2_r, y1_s, y1_r, x2_s, x2_r,
    zx_s, zx_r, zy_s, zy_r, i_s, i_r,
):
    s = lax.axis_index("space")
    l = lax.axis_index("chan")
    core = lax.rem(s, 2)
    z = lax.rem(lax.div(s, 2), NZ)
    x = lax.rem(lax.div(s, 2 * NZ), NX)
    y = lax.div(s, 2 * NZ * NX)
    count = 2 * NZ * NX * NY

    partner = (device(y, x, z, 1 - core), l)
    outer = (lax.rem(s + 2 * core - 1 + count, count), l)
    x_peers = [(device(y, lax.rem(x + d, NX), z, core), l) for d in range(1, NX)]
    y_peer = (device(1 - y, x, z, core), l)
    z_peers = [(device(y, x, lax.rem(z + d, NZ), core), l) for d in range(1, NZ)]
    chan_peer = (s, 1 - l)

    sent = []

    def send(src, dst, ss, rs, to):
        copy = pltpu.make_async_remote_copy(
            src_ref=src, dst_ref=dst, send_sem=ss, recv_sem=rs, device_id=to, device_id_type=MESH
        )
        copy.start()
        sent.append(copy)
        return copy

    first = 1 + 2 * core
    here = pl.ds(first, 2)
    load_f = pltpu.make_async_copy(feat, fb.at[here], loc.at[0])
    load_f.start()
    load_k = []
    for n, t0 in enumerate((9, 0, 18)):
        part = pl.ds(t0, 9)
        load_k.append(pltpu.make_async_copy(kern.at[part], kv.at[part], loc.at[1 + n]))
    for copy in load_k:
        copy.start()
    load_c = pltpu.make_async_copy(cot, ct, loc.at[4])
    load_c.start()

    barrier = pltpu.get_barrier_semaphore()
    greeted = [partner, outer, *x_peers, y_peer, *z_peers, chan_peer]
    for peer in greeted:
        pl.semaphore_signal(barrier, inc=1, device_id=peer, device_id_type=MESH)

    pl.semaphore_wait(barrier, len(greeted))

    f_out = send(feat.at[core], fb.at[5 * (1 - core)], f_s.at[0], f_r.at[0], outer)
    f_pair = send(feat, fb.at[here], f_s.at[1], f_r.at[1], partner)

    def spread_f(slot, plane):
        def store(ci, part):
            fs[ci, slot, SZ : SZ + CELLS, :] = part
            fs[ci, slot, 0:SZ, :] = part[CELLS - SZ :]
            fs[ci, slot, SZ + CELLS :, :] = part[:SZ]

        spread(plane, -1, store)

    def spread_g(g):
        def store(ci, part):
            ps[ci, g, SZ : SZ + CELLS, :] = part
            ps[ci, g, 0:SZ, :] = part[CELLS - SZ :]
            ps[ci, g, SZ + CELLS :, :] = part[:SZ]

        spread(pr[g], 1, store)

    def taps_f(slot):
        return jnp.concatenate(
            [fs[c, slot, b * SZ : b * SZ + CELLS, :] for b in range(3) for c in range(3)], axis=1
        )

    def times(slot, t0):
        return jnp.dot(taps_f(slot), kv[pl.ds(t0, 9)].reshape(9 * C, C), preferred_element_type=F32)

    row = lax.broadcasted_iota(jnp.int32, (HALF, C), 0)
    col = lax.broadcasted_iota(jnp.int32, (HALF, C), 1)
    sel[...] = jnp.where((row >> 1) * 4 + core * 2 + (row & 1) == col, 1.0, 0.0).astype(BF)

    load_f.wait()
    for i in range(2):
        spread_f(1 + i, fb[first + i])
    load_k[0].wait()
    for i in range(2):
        acc[i] = times(1 + i, 9)
    load_k[1].wait()
    acc[1] += times(1, 0)
    load_k[2].wait()
    acc[0] += times(2, 18)
    load_c.wait()

    def epilogue(i, g):
        def body(n, carry):
            rows = pl.ds(pl.multiple_of(n * 64, 64), 64)
            pre = acc[i, rows, :]
            sig = 1.0 / (1.0 + jnp.exp(-pre))
            pr[g, rows, :] = (ct[i, rows, :].astype(F32) * sig * (1.0 + pre * (1.0 - sig))).astype(BF)
            return carry

        lax.fori_loop(0, CELLS // 64, body, 0)

    def features_t(g):
        cols = pl.ds(pl.multiple_of(g * CELLS, CELLS), CELLS)
        ft[:, cols] = lax.dot_general(sel[...], fb[g], NT, preferred_element_type=F32).astype(BF)

    f_pair.wait_recv()
    side = 3 * (1 - core)
    spread_f(side, fb[2 * core + side])
    inner = 1 - core
    acc[inner] += times(side, 18 * (1 - core))
    g_inner = 2 + core
    epilogue(inner, g_inner)
    g_pair0 = send(pr.at[g_inner], pr.at[g_inner], g_s.at[0], g_r.at[0], partner)

    f_out.wait_recv()
    f_relay = send(fb.at[5 * core], fb.at[5 * core], f_s.at[2], f_r.at[2], partner)
    spread_f(3 * core, fb[5 * core])
    acc[core] += times(3 * core, 18 * core)
    g_outer = 1 + 3 * core
    epilogue(core, g_outer)
    g_pair1 = send(pr.at[g_outer], pr.at[g_outer], g_s.at[1], g_r.at[1], partner)
    g_out = send(pr.at[g_outer], pr.at[5 * (1 - core)], g_s.at[2], g_r.at[2], outer)
    spread_g(g_inner)
    spread_g(g_outer)
    for g in range(1, 5):
        features_t(g)
    features_t(5 * core)
    f_relay.wait_recv()
    features_t(5 * (1 - core))
    g_pair0.wait_recv()
    spread_g(3 - core)
    g_pair1.wait_recv()
    spread_g(4 - 3 * core)

    first_x, first_y = {}, {}
    for g in ORDER:
        b, c = divmod(g, 3)
        left = jnp.concatenate([ft[:, a * CELLS : (a + 4) * CELLS] for a in range(3)], axis=0)
        right = jnp.concatenate(
            [ps[c, p, (2 - b) * SZ : (2 - b) * SZ + CELLS, :] for p in range(1, 5)], axis=0
        )
        part = jnp.dot(left, right, preferred_element_type=F32).astype(BF)
        part = part.reshape(3, NY, NX, 16, C)
        if g in X_SET:
            n = X_SET.index(g)
            for k in range(NX):
                pkx[n, k] = part[:, :, k]
            first_x[n] = [
                send(pkx.at[n, lax.rem(x + d, NX)], xr1.at[n, d - 1], x1_s.at[n, d - 1], x1_r.at[n, d - 1], x_peers[d - 1])
                for d in range(1, NX)
            ]
        else:
            n = Y_SET.index(g)
            for k in range(NY):
                pky[n, k] = part[:, k]
            first_y[n] = send(pky.at[n, 1 - y], yr1.at[n], y1_s.at[n], y1_r.at[n], y_peer)

    second_x, second_y = {}, {}

    def sum_x1(n):
        for copy in first_x[n]:
            copy.wait_recv()
        total = pkx[n, x].astype(F32)
        for d in range(NX - 1):
            total = total + xr1[n, d].astype(F32)
        total = total.astype(BF)
        for k in range(NY):
            s1x[n, k] = total[:, k]
        second_x[n] = send(s1x.at[n, 1 - y], yr2.at[n], y2_s.at[n], y2_r.at[n], y_peer)

    def sum_y1(n):
        first_y[n].wait_recv()
        total = (pky[n, y].astype(F32) + yr1[n].astype(F32)).astype(BF)
        for k in range(NX):
            s1y[n, k] = total[:, k]
        second_y[n] = [
            send(s1y.at[n, lax.rem(x + d, NX)], xr2.at[n, d - 1], x2_s.at[n, d - 1], x2_r.at[n, d - 1], x_peers[d - 1])
            for d in range(1, NX)
        ]

    def sum_x2(n):
        second_x[n].wait_recv()
        total = s1x[n, y].astype(F32) + yr2[n].astype(F32)
        s2x[n * 48 : (n + 1) * 48, :] = total.astype(BF).reshape(48, C)

    def sum_y2(n):
        for copy in second_y[n]:
            copy.wait_recv()
        total = s1y[n, x].astype(F32)
        for d in range(NX - 1):
            total = total + xr2[n, d].astype(F32)
        s2y[n * 48 : (n + 1) * 48, :] = total.astype(BF).reshape(48, C)

    def ordered(perm, rows, out):
        out[...] = jnp.dot(perm[...], rows[...], preferred_element_type=F32).astype(BF).reshape(out.shape)

    def last(perm, rows, zs, zr, ss, rs):
        ordered(perm, rows, zs)
        return [
            send(zs.at[lax.rem(z + d, NZ)], zr.at[d - 1], ss.at[d - 1], rs.at[d - 1], z_peers[d - 1])
            for d in range(1, NZ)
        ]

    def input_plane(i):
        total = None
        for a in range(3):
            left = jnp.concatenate(
                [ps[c, first + i - (a - 1), (2 - b) * SZ : (2 - b) * SZ + CELLS, :] for b in range(3) for c in range(3)],
                axis=1,
            )
            right = jnp.concatenate([kv[9 * a + u] for u in range(9)], axis=1)
            term = lax.dot_general(left, right, NT, preferred_element_type=F32)
            total = term if total is None else total + term
        low, high = total[:, :HALF], total[:, HALF:]
        own[i] = jnp.where(l == 0, low, high)
        igs[i] = jnp.where(l == 0, high, low).astype(BF)

    row = lax.broadcasted_iota(jnp.int32, (C, C), 0)
    col = lax.broadcasted_iota(jnp.int32, (C, C), 1)
    for perm, groups, shift in ((permx, X_SET, BX), (permy, Y_SET, BY)):
        n = len(groups)
        block = lax.div(row, shift)
        q = row - block * shift
        a = jnp.where(q >= 2 * n, 1, 0) + jnp.where(q >= 4 * n, 1, 0)
        rest = q - 2 * n * a
        source = ((rest >> 1) * 3 + a) * 16 + block * 2 + (rest & 1)
        hot = jnp.where((source == col) & (q < 6 * n), 1.0, 0.0).astype(BF)
        perm[...] = hot[: 8 * shift]
    s2x[...] = jnp.zeros_like(s2x)
    s2y[...] = jnp.zeros_like(s2y)

    g_out.wait_recv()
    spread_g(5 * core)
    input_plane(0)
    for n in range(3):
        sum_y1(n)
    for n in range(2):
        sum_x1(n)
    input_plane(1)
    for n in range(2, 4):
        sum_x1(n)
    for n in range(3, 5):
        sum_y1(n)
    ig_copies = [send(igs.at[i], igr.at[i], i_s.at[i], i_r.at[i], chan_peer) for i in range(2)]
    for n in range(4):
        sum_x2(n)
    copies_x = last(permx, s2x, zsx, zrx, zx_s, zx_r)
    for n in range(5):
        sum_y2(n)
    copies_y = last(permy, s2y, zsy, zry, zy_s, zy_r)

    def final(groups, copies, mine, taken):
        total = mine.astype(F32)
        for d, copy in enumerate(copies):
            copy.wait_recv()
            total = total + taken[d].astype(F32)
        n = len(groups)
        for a in range(3):
            kg_sum[a * 9 + groups[0] : a * 9 + groups[0] + n] = total[a * 2 * n : (a + 1) * 2 * n].reshape(n, 2, C)

    out_copies = []
    for i, copy in enumerate(ig_copies):
        copy.wait_recv()
        ig_sum[i] = (own[i] + igr[i].astype(F32)).astype(BF)
        out_copies.append(pltpu.make_async_copy(ig_sum.at[i], ig_out.at[i], loc.at[5 + i]))
        out_copies[-1].start()
    final(Y_SET, copies_y, zsy[z], zry)
    final(X_SET, copies_x, zsx[z], zrx)
    out_copies.append(pltpu.make_async_copy(kg_sum, kg_out, loc.at[7]))
    out_copies[-1].start()
    for copy in out_copies:
        copy.wait()

    for copy in sent:
        copy.wait_send()


def copy_out(ig, kg, ig_out, kg_out, ig_held, kg_held, sem):
    steps = []
    for i in range(2):
        for h in range(2):
            part = (i, pl.ds(h * (CELLS // 2), CELLS // 2))
            steps.append((ig.at[part], ig_held.at[part], ig_out.at[part]))
    steps.append((kg, kg_held, kg_out))
    copies = [
        (pltpu.make_async_copy(a, b, sem.at[0, n]), pltpu.make_async_copy(b, c, sem.at[1, n]))
        for n, (a, b, c) in enumerate(steps)
    ]
    for inward, _ in copies:
        inward.start()
    for inward, outward in copies:
        inward.wait()
        outward.start()
    for _, outward in copies:
        outward.wait()


def shards(features, kernel, cotangent):
    taps = jnp.transpose(kernel, (1, 0, 2))
    dma = pltpu.SemaphoreType.DMA
    nx, ny = len(X_SET), len(Y_SET)
    pairs = [(3,), (3,), (nx, 3), (nx,), (ny,), (ny, 3), (7,), (7,), (2,)]
    sems = [dma((8,))]
    for shape in pairs:
        sems += [dma(shape), dma(shape)]
    whole = pl.BlockSpec(memory_space=pl.ANY)
    input_grad, kernel_grad = pl.pallas_call(
        fused,
        name="conv_grads",
        out_shape=(
            jax.ShapeDtypeStruct((2, CELLS, HALF), BF),
            jax.ShapeDtypeStruct((27, 2, C), F32),
        ),
        in_specs=[whole] * 3,
        out_specs=(whole, whole),
        scratch_shapes=[
            pltpu.VMEM((27, C, C), BF),
            pltpu.VMEM((6, CELLS, C), BF),
            pltpu.VMEM((2, CELLS, C), BF),
            pltpu.VMEM((3, 4, HALO, C), BF),
            pltpu.VMEM((6, CELLS, C), BF),
            pltpu.VMEM((3, 6, HALO, C), BF),
            pltpu.VMEM((HALF, 6 * CELLS), BF),
            pltpu.VMEM((2, CELLS, C), F32),
            pltpu.VMEM((nx, NX, 3, NY, 16, C), BF),
            pltpu.VMEM((ny, NY, 3, NX, 16, C), BF),
            pltpu.VMEM((nx, 3, 3, NY, 16, C), BF),
            pltpu.VMEM((nx, NY, 3, 16, C), BF),
            pltpu.VMEM((nx, 3, 16, C), BF),
            pltpu.VMEM((ny, 3, NX, 16, C), BF),
            pltpu.VMEM((ny, NX, 3, 16, C), BF),
            pltpu.VMEM((ny, 3, 3, 16, C), BF),
            pltpu.VMEM((C, C), BF),
            pltpu.VMEM((C, C), BF),
            pltpu.VMEM((NZ, BX, C), BF),
            pltpu.VMEM((NZ, BY, C), BF),
            pltpu.VMEM((NZ - 1, BX, C), BF),
            pltpu.VMEM((NZ - 1, BY, C), BF),
            pltpu.VMEM((2, CELLS, HALF), F32),
            pltpu.VMEM((2, CELLS, HALF), BF),
            pltpu.VMEM((2, CELLS, HALF), BF),
            pltpu.VMEM((8 * BX, C), BF),
            pltpu.VMEM((8 * BY, C), BF),
            pltpu.VMEM((HALF, C), BF),
            pltpu.VMEM((2, CELLS, HALF), BF),
            pltpu.VMEM((27, 2, C), F32),
            *sems,
        ],
        compiler_params=pltpu.CompilerParams(
            collective_id=0, has_side_effects=True, vmem_limit_bytes=58 * 1024 * 1024
        ),
        cost_estimate=pl.CostEstimate(flops=11_000_000_000, bytes_accessed=6_000_000, transcendentals=300_000),
    )(features.reshape(2, CELLS, C), taps, cotangent.reshape(2, CELLS, C))
    input_grad, kernel_grad = pl.pallas_call(
        copy_out,
        name="copy_out",
        out_shape=(
            jax.ShapeDtypeStruct((2, CELLS, HALF), BF),
            jax.ShapeDtypeStruct((27, 2, C), F32),
        ),
        in_specs=[whole] * 2,
        out_specs=(whole, whole),
        scratch_shapes=[
            pltpu.VMEM((2, CELLS, HALF), BF),
            pltpu.VMEM((27, 2, C), F32),
            dma((2, 5)),
        ],
        compiler_params=pltpu.CompilerParams(vmem_limit_bytes=60 * 1024 * 1024),
    )(input_grad, kernel_grad)
    return (
        input_grad.reshape(2, SY, SZ, HALF),
        jnp.transpose(kernel_grad, (1, 0, 2)),
    )


def solution(mesh):
    placed = (P("space", None, None, None), P(None, None, "chan"), P("space", None, None, "chan"))
    return jax.shard_map(
        shards,
        mesh=mesh,
        in_specs=placed,
        out_specs=(P("space", None, None, "chan"), P("space", None, "chan")),
        check_vma=False,
    )
```

profile of v0, /device:TPU:32, one launch (start us, length us, event | category | flops | bytes accessed | tf_op | source)
XLA Modules:
  0.0 51.0 jit_solution(18430490869955106276)
XLA Ops:
  0.6 48.5 %conv_grads.1 = (bf16[2,512,128]{2,1,0:T(8,128)(2,1)}, f32[27,2,256]{2,1,0:T(2,128)}) custom-call(bf16[2,512,256]{2,1,0:T(8,128)(2,1)} %bitcast.6, bf16[27,256,256]{2,1,0:T(8,128)(2,1)} %bitcast.5, bf16[2,512,256]{2,1,0:T(8,128)(2,1)} %bitcast.7), custom_call_target="tpu_custom_call" | custom-call | flops 11000000512 | bytes 6000000 | tf_op jit(solution)/shard_map/conv_grads/pallas_call | solution.py:356
  49.2 1.7 %copy_out.1 = (bf16[2,512,128]{2,1,0:T(8,128)(2,1)}, f32[27,2,256]{2,1,0:T(2,128)}) custom-call(bf16[2,512,128]{2,1,0:T(8,128)(2,1)} %get-tuple-element.6.ig, f32[27,2,256]{2,1,0:T(2,128)} %get-tuple-element.7.kg), custom_call_target="tpu_custom_call" | custom-call | tf_op jit(solution)/shard_map/copy_out/pallas_call | solution.py:403
where the time goes:
time: 51.6 us; the launch traced here: 51 us
  Pallas kernels  50.2 us (97%)
  between operations  0.8 us (2%)
    pallas_call x1, Pallas kernels, shards(): pl.pallas_call(fused, name='conv_grads', out_shape=(jax.ShapeDtypeStruct(...  48.5 us
    pallas_call x1, Pallas kernels, shards(): pl.pallas_call(copy_out, name='copy_out', out_shape=(jax.ShapeDtypeStruct...  1.67 us

commit v1 on v0

--- a/solution.py
+++ b/solution.py
@@ -17,7 +17,6 @@
 
 Y_SET = (0, 1, 2, 3, 4)
 X_SET = (5, 6, 7, 8)
-ORDER = (0, 5, 1, 6, 2, 7, 3, 8, 4)
 
 NT = (((1,), (1,)), ((), ()))
 
@@ -43,7 +42,7 @@
 
 def fused(
     feat, kern, cot, ig_out, kg_out,
-    kv, fb, ct, fs, pr, ps, ft, acc, pkx, pky,
+    kv, fb, ct, fs, pr, ps, ft, acc, pk,
     xr1, s1x, yr2, yr1, s1y, xr2, s2x, s2y, zsx, zsy, zrx, zry,
     own, igs, igr, permx, permy, sel,
     ig_sum, kg_sum,
@@ -71,8 +70,12 @@
         copy = pltpu.make_async_remote_copy(
             src_ref=src, dst_ref=dst, send_sem=ss, recv_sem=rs, device_id=to, device_id_type=MESH
         )
+        sent.append(copy)
+        return copy
+
+    def start(*args):
+        copy = send(*args)
         copy.start()
-        sent.append(copy)
         return copy
 
     first = 1 + 2 * core
@@ -95,8 +98,8 @@
 
     pl.semaphore_wait(barrier, len(greeted))
 
-    f_out = send(feat.at[core], fb.at[5 * (1 - core)], f_s.at[0], f_r.at[0], outer)
-    f_pair = send(feat, fb.at[here], f_s.at[1], f_r.at[1], partner)
+    f_out = start(feat.at[core], fb.at[5 * (1 - core)], f_s.at[0], f_r.at[0], outer)
+    f_pair = start(feat, fb.at[here], f_s.at[1], f_r.at[1], partner)
 
     def spread_f(slot, plane):
         def store(ci, part):
@@ -108,11 +111,15 @@
 
     def spread_g(g):
         def store(ci, part):
-            ps[ci, g, SZ : SZ + CELLS, :] = part
-            ps[ci, g, 0:SZ, :] = part[CELLS - SZ :]
-            ps[ci, g, SZ + CELLS :, :] = part[:SZ]
+            part = part.reshape(SY, SZ, C)
+            ps[ci, g, 1 : SY + 1] = part
+            ps[ci, g, 0] = part[SY - 1]
+            ps[ci, g, SY + 1] = part[0]
 
         spread(pr[g], 1, store)
+
+    def taps_g(c, g, b):
+        return ps[c, g, pl.ds(2 - b, SY)].reshape(CELLS, C)
 
     def taps_f(slot):
         return jnp.concatenate(
@@ -129,14 +136,7 @@
     load_f.wait()
     for i in range(2):
         spread_f(1 + i, fb[first + i])
-    load_k[0].wait()
-    for i in range(2):
-        acc[i] = times(1 + i, 9)
-    load_k[1].wait()
-    acc[1] += times(1, 0)
-    load_k[2].wait()
-    acc[0] += times(2, 18)
-    load_c.wait()
+    acc[...] = jnp.zeros_like(acc)
 
     def epilogue(i, g):
         def body(n, carry):
@@ -152,23 +152,66 @@
         cols = pl.ds(pl.multiple_of(g * CELLS, CELLS), CELLS)
         ft[:, cols] = lax.dot_general(sel[...], fb[g], NT, preferred_element_type=F32).astype(BF)
 
-    f_pair.wait_recv()
-    side = 3 * (1 - core)
-    spread_f(side, fb[2 * core + side])
     inner = 1 - core
-    acc[inner] += times(side, 18 * (1 - core))
-    g_inner = 2 + core
-    epilogue(inner, g_inner)
+    side = 3 * inner
+    g_inner, g_outer, g_far = 2 + core, 1 + 3 * core, 5 * core
+    g_side = 2 * core + side
+    f_relay = send(fb.at[g_far], fb.at[g_far], f_s.at[2], f_r.at[2], partner)
     g_pair0 = send(pr.at[g_inner], pr.at[g_inner], g_s.at[0], g_r.at[0], partner)
-
-    f_out.wait_recv()
-    f_relay = send(fb.at[5 * core], fb.at[5 * core], f_s.at[2], f_r.at[2], partner)
-    spread_f(3 * core, fb[5 * core])
-    acc[core] += times(3 * core, 18 * core)
-    g_outer = 1 + 3 * core
-    epilogue(core, g_outer)
     g_pair1 = send(pr.at[g_outer], pr.at[g_outer], g_s.at[1], g_r.at[1], partner)
-    g_out = send(pr.at[g_outer], pr.at[5 * (1 - core)], g_s.at[2], g_r.at[2], outer)
+    g_out = send(pr.at[g_outer], pr.at[5 * inner], g_s.at[2], g_r.at[2], outer)
+
+    def forward(n, carry):
+        late = n // 4
+        m = n % 4
+        slot = (1 - late) * (1 + n % 2) + late * ((1 - m) * side + m * 3 * core)
+        t0 = (1 - late) * (9 + (n // 2) * (18 * (n % 2) - 9)) + late * 18 * ((1 - m) * inner + m * core)
+        i = (1 - late) * ((n % 2 + n // 2) % 2) + late * ((1 - m) * inner + m * core)
+
+        @pl.when(n == 0)
+        def _():
+            load_k[0].wait()
+
+        @pl.when(n == 2)
+        def _():
+            load_k[1].wait()
+
+        @pl.when(n == 3)
+        def _():
+            load_k[2].wait()
+
+        @pl.when(n == 4)
+        def _():
+            load_c.wait()
+            f_pair.wait_recv()
+
+        @pl.when(n == 5)
+        def _():
+            f_out.wait_recv()
+            f_relay.start()
+
+        @pl.when(n >= 4)
+        def _():
+            spread_f(slot, fb[2 * core + slot])
+
+        acc[i] += times(slot, t0)
+
+        @pl.when(n >= 4)
+        def _():
+            epilogue(i, first + i)
+
+        @pl.when(n == 4)
+        def _():
+            g_pair0.start()
+
+        @pl.when(n == 5)
+        def _():
+            g_pair1.start()
+            g_out.start()
+
+        return carry
+
+    lax.fori_loop(0, 6, forward, 0)
     spread_g(g_inner)
     spread_g(g_outer)
     for g in range(1, 5):
@@ -181,63 +224,85 @@
     g_pair1.wait_recv()
     spread_g(4 - 3 * core)
 
-    first_x, first_y = {}, {}
-    for g in ORDER:
-        b, c = divmod(g, 3)
+    def remote(src, dst, ss, rs, to):
+        return pltpu.make_async_remote_copy(
+            src_ref=src, dst_ref=dst, send_sem=ss, recv_sem=rs, device_id=to, device_id_type=MESH
+        )
+
+    def x1(n, d):
+        mine = pk.at[2 * n + 1, :, :, lax.rem(x + d, NX)]
+        return remote(mine, xr1.at[n, d - 1], x1_s.at[n, d - 1], x1_r.at[n, d - 1], x_peers[d - 1])
+
+    def y1(n):
+        return remote(pk.at[2 * n, :, 1 - y], yr1.at[n], y1_s.at[n], y1_r.at[n], y_peer)
+
+    def x2(n, d):
+        mine = s1y.at[n, lax.rem(x + d, NX)]
+        return remote(mine, xr2.at[n, d - 1], x2_s.at[n, d - 1], x2_r.at[n, d - 1], x_peers[d - 1])
+
+    def y2(n):
+        return remote(s1x.at[n, 1 - y], yr2.at[n], y2_s.at[n], y2_r.at[n], y_peer)
+
+    def terms(u, carry):
+        odd = u % 2
+        n = u // 2
+        g = n + len(Y_SET) * odd
+        b = g // 3
+        c = g % 3
         left = jnp.concatenate([ft[:, a * CELLS : (a + 4) * CELLS] for a in range(3)], axis=0)
-        right = jnp.concatenate(
-            [ps[c, p, (2 - b) * SZ : (2 - b) * SZ + CELLS, :] for p in range(1, 5)], axis=0
-        )
-        part = jnp.dot(left, right, preferred_element_type=F32).astype(BF)
-        part = part.reshape(3, NY, NX, 16, C)
-        if g in X_SET:
-            n = X_SET.index(g)
-            for k in range(NX):
-                pkx[n, k] = part[:, :, k]
-            first_x[n] = [
-                send(pkx.at[n, lax.rem(x + d, NX)], xr1.at[n, d - 1], x1_s.at[n, d - 1], x1_r.at[n, d - 1], x_peers[d - 1])
-                for d in range(1, NX)
-            ]
-        else:
-            n = Y_SET.index(g)
-            for k in range(NY):
-                pky[n, k] = part[:, k]
-            first_y[n] = send(pky.at[n, 1 - y], yr1.at[n], y1_s.at[n], y1_r.at[n], y_peer)
-
-    second_x, second_y = {}, {}
+        right = jnp.concatenate([taps_g(c, p, b) for p in range(1, 5)], axis=0)
+        pk[u] = jnp.dot(left, right, preferred_element_type=F32).astype(BF).reshape(3, NY, NX, 16, C)
+
+        @pl.when(odd == 0)
+        def _():
+            y1(n).start()
+
+        @pl.when(odd == 1)
+        def _():
+            for d in range(1, NX):
+                x1(n, d).start()
+
+        return carry
+
+    lax.fori_loop(0, 9, terms, 0)
 
     def sum_x1(n):
-        for copy in first_x[n]:
-            copy.wait_recv()
-        total = pkx[n, x].astype(F32)
-        for d in range(NX - 1):
-            total = total + xr1[n, d].astype(F32)
+        total = pk[2 * n + 1, :, :, x].astype(F32)
+        for d in range(1, NX):
+            x1(n, d).wait_recv()
+            total = total + xr1[n, d - 1].astype(F32)
         total = total.astype(BF)
         for k in range(NY):
             s1x[n, k] = total[:, k]
-        second_x[n] = send(s1x.at[n, 1 - y], yr2.at[n], y2_s.at[n], y2_r.at[n], y_peer)
+        y2(n).start()
 
     def sum_y1(n):
-        first_y[n].wait_recv()
-        total = (pky[n, y].astype(F32) + yr1[n].astype(F32)).astype(BF)
+        y1(n).wait_recv()
+        total = (pk[2 * n, :, y].astype(F32) + yr1[n].astype(F32)).astype(BF)
         for k in range(NX):
             s1y[n, k] = total[:, k]
-        second_y[n] = [
-            send(s1y.at[n, lax.rem(x + d, NX)], xr2.at[n, d - 1], x2_s.at[n, d - 1], x2_r.at[n, d - 1], x_peers[d - 1])
-            for d in range(1, NX)
-        ]
+        for d in range(1, NX):
+            x2(n, d).start()
+
+    def sum_1(n, carry):
+        sum_y1(n)
+
+        @pl.when(n < len(X_SET))
+        def _():
+            sum_x1(n)
+
+        return carry
 
     def sum_x2(n):
-        second_x[n].wait_recv()
+        y2(n).wait_recv()
         total = s1x[n, y].astype(F32) + yr2[n].astype(F32)
         s2x[n * 48 : (n + 1) * 48, :] = total.astype(BF).reshape(48, C)
 
     def sum_y2(n):
-        for copy in second_y[n]:
-            copy.wait_recv()
         total = s1y[n, x].astype(F32)
-        for d in range(NX - 1):
-            total = total + xr2[n, d].astype(F32)
+        for d in range(1, NX):
+            x2(n, d).wait_recv()
+            total = total + xr2[n, d - 1].astype(F32)
         s2y[n * 48 : (n + 1) * 48, :] = total.astype(BF).reshape(48, C)
 
     def ordered(perm, rows, out):
@@ -246,23 +311,22 @@
     def last(perm, rows, zs, zr, ss, rs):
         ordered(perm, rows, zs)
         return [
-            send(zs.at[lax.rem(z + d, NZ)], zr.at[d - 1], ss.at[d - 1], rs.at[d - 1], z_peers[d - 1])
+            start(zs.at[lax.rem(z + d, NZ)], zr.at[d - 1], ss.at[d - 1], rs.at[d - 1], z_peers[d - 1])
             for d in range(1, NZ)
         ]
 
-    def input_plane(i):
-        total = None
-        for a in range(3):
-            left = jnp.concatenate(
-                [ps[c, first + i - (a - 1), (2 - b) * SZ : (2 - b) * SZ + CELLS, :] for b in range(3) for c in range(3)],
-                axis=1,
-            )
-            right = jnp.concatenate([kv[9 * a + u] for u in range(9)], axis=1)
-            term = lax.dot_general(left, right, NT, preferred_element_type=F32)
-            total = term if total is None else total + term
-        low, high = total[:, :HALF], total[:, HALF:]
-        own[i] = jnp.where(l == 0, low, high)
-        igs[i] = jnp.where(l == 0, high, low).astype(BF)
+    def input_part(n, carry):
+        i = n // 3
+        a = n % 3
+        left = jnp.concatenate([taps_g(c, first + i + 1 - a, b) for b in range(3) for c in range(3)], axis=1)
+        right = jnp.concatenate([kv[9 * a + u] for u in range(9)], axis=1)
+
+        @pl.when(a == 0)
+        def _():
+            acc[i] = jnp.zeros((CELLS, C), F32)
+
+        acc[i] += lax.dot_general(left, right, NT, preferred_element_type=F32)
+        return carry
 
     row = lax.broadcasted_iota(jnp.int32, (C, C), 0)
     col = lax.broadcasted_iota(jnp.int32, (C, C), 1)
@@ -280,17 +344,13 @@
 
     g_out.wait_recv()
     spread_g(5 * core)
-    input_plane(0)
-    for n in range(3):
-        sum_y1(n)
-    for n in range(2):
-        sum_x1(n)
-    input_plane(1)
-    for n in range(2, 4):
-        sum_x1(n)
-    for n in range(3, 5):
-        sum_y1(n)
-    ig_copies = [send(igs.at[i], igr.at[i], i_s.at[i], i_r.at[i], chan_peer) for i in range(2)]
+    lax.fori_loop(0, 6, input_part, 0)
+    for i in range(2):
+        low, high = acc[i, :, :HALF], acc[i, :, HALF:]
+        own[i] = jnp.where(l == 0, low, high)
+        igs[i] = jnp.where(l == 0, high, low).astype(BF)
+    lax.fori_loop(0, len(Y_SET), sum_1, 0)
+    ig_copies = [start(igs.at[i], igr.at[i], i_s.at[i], i_r.at[i], chan_peer) for i in range(2)]
     for n in range(4):
         sum_x2(n)
     copies_x = last(permx, s2x, zsx, zrx, zx_s, zx_r)
@@ -322,6 +382,21 @@
 
     for copy in sent:
         copy.wait_send()
+
+    def drain(n, carry):
+        y1(n).wait_send()
+        for d in range(1, NX):
+            x2(n, d).wait_send()
+
+        @pl.when(n < len(X_SET))
+        def _():
+            y2(n).wait_send()
+            for d in range(1, NX):
+                x1(n, d).wait_send()
+
+        return carry
+
+    lax.fori_loop(0, len(Y_SET), drain, 0)
 
 
 def copy_out(ig, kg, ig_out, kg_out, ig_held, kg_held, sem):
@@ -368,11 +443,10 @@
             pltpu.VMEM((2, CELLS, C), BF),
             pltpu.VMEM((3, 4, HALO, C), BF),
             pltpu.VMEM((6, CELLS, C), BF),
-            pltpu.VMEM((3, 6, HALO, C), BF),
+            pltpu.VMEM((3, 6, SY + 2, SZ, C), BF),
             pltpu.VMEM((HALF, 6 * CELLS), BF),
             pltpu.VMEM((2, CELLS, C), F32),
-            pltpu.VMEM((nx, NX, 3, NY, 16, C), BF),
-            pltpu.VMEM((ny, NY, 3, NX, 16, C), BF),
+            pltpu.VMEM((9, 3, NY, NX, 16, C), BF),
             pltpu.VMEM((nx, 3, 3, NY, 16, C), BF),
             pltpu.VMEM((nx, NY, 3, 16, C), BF),
             pltpu.VMEM((nx, 3, 16, C), BF),

time: 51.6 us -> 47.6 us (0.922)
  Pallas kernels: 50.2 us -> 46.8 us
    pallas_call x1, Pallas kernels: 48.5 us -> 45.2 us  [shards(): pl.pallas_call(fused, name='conv_grads', out_shape=(jax.ShapeDtypeStruct(...]
where the time goes in v1:
time: 47.6 us; the launch traced here: 47.5 us
  Pallas kernels  46.8 us (98%)
  between operations  0.64 us (1%)
    pallas_call x1, Pallas kernels, shards(): pl.pallas_call(fused, name='conv_grads', out_shape=(jax.ShapeDtypeStruct(...  45.2 us
    pallas_call x1, Pallas kernels, shards(): pl.pallas_call(copy_out, name='copy_out', out_shape=(jax.ShapeDtypeStruct...  1.67 us

profile of v1, /device:TPU:32, one launch (start us, length us, event | category | flops | bytes accessed | tf_op | source)
XLA Modules:
  0.0 47.5 jit_solution(14124114839457424815)
XLA Ops:
  0.6 45.2 %conv_grads.1 = (bf16[2,512,128]{2,1,0:T(8,128)(2,1)}, f32[27,2,256]{2,1,0:T(2,128)}) custom-call(bf16[2,512,256]{2,1,0:T(8,128)(2,1)} %bitcast.6, bf16[27,256,256]{2,1,0:T(8,128)(2,1)} %bitcast.5, bf16[2,512,256]{2,1,0:T(8,128)(2,1)} %bitcast.7), custom_call_target="tpu_custom_call" | custom-call | flops 11000000512 | bytes 6000000 | tf_op jit(solution)/shard_map/conv_grads/pallas_call | solution.py:431
  45.8 1.7 %copy_out.1 = (bf16[2,512,128]{2,1,0:T(8,128)(2,1)}, f32[27,2,256]{2,1,0:T(2,128)}) custom-call(bf16[2,512,128]{2,1,0:T(8,128)(2,1)} %get-tuple-element.6.ig, f32[27,2,256]{2,1,0:T(2,128)} %get-tuple-element.7.kg), custom_call_target="tpu_custom_call" | custom-call | tf_op jit(solution)/shard_map/copy_out/pallas_call | solution.py:477

commit v2 on v1

--- a/solution.py
+++ b/solution.py
@@ -310,10 +310,13 @@
 
     def last(perm, rows, zs, zr, ss, rs):
         ordered(perm, rows, zs)
-        return [
-            start(zs.at[lax.rem(z + d, NZ)], zr.at[d - 1], ss.at[d - 1], rs.at[d - 1], z_peers[d - 1])
+        copies = [
+            send(zs.at[lax.rem(z + d, NZ)], zr.at[d - 1], ss.at[d - 1], rs.at[d - 1], z_peers[d - 1])
             for d in range(1, NZ)
         ]
+        for d in (4, 3, 5, 2, 6, 1, 7):
+            copies[d - 1].start()
+        return copies
 
     def input_part(n, carry):
         i = n // 3

time: 47.6 us -> 47.5 us (level)
  no operation moved by 1% of the time
where the time goes in v2:
time: 47.5 us; the launch traced here: 47.4 us
  Pallas kernels  46.7 us (98%)
  between operations  0.64 us (1%)
    pallas_call x1, Pallas kernels, shards(): pl.pallas_call(fused, name='conv_grads', out_shape=(jax.ShapeDtypeStruct(...  45.1 us
    pallas_call x1, Pallas kernels, shards(): pl.pallas_call(copy_out, name='copy_out', out_shape=(jax.ShapeDtypeStruct...  1.67 us

profile of v2, /device:TPU:32, one launch (start us, length us, event | category | flops | bytes accessed | tf_op | source)
XLA Modules:
  0.0 47.4 jit_solution(1157010913685328458)
XLA Ops:
  0.6 45.1 %conv_grads.1 = (bf16[2,512,128]{2,1,0:T(8,128)(2,1)}, f32[27,2,256]{2,1,0:T(2,128)}) custom-call(bf16[2,512,256]{2,1,0:T(8,128)(2,1)} %bitcast.6, bf16[27,256,256]{2,1,0:T(8,128)(2,1)} %bitcast.5, bf16[2,512,256]{2,1,0:T(8,128)(2,1)} %bitcast.7), custom_call_target="tpu_custom_call" | custom-call | flops 11000000512 | bytes 6000000 | tf_op jit(solution)/shard_map/conv_grads/pallas_call | solution.py:434
  45.7 1.7 %copy_out.1 = (bf16[2,512,128]{2,1,0:T(8,128)(2,1)}, f32[27,2,256]{2,1,0:T(2,128)}) custom-call(bf16[2,512,128]{2,1,0:T(8,128)(2,1)} %get-tuple-element.6.ig, f32[27,2,256]{2,1,0:T(2,128)} %get-tuple-element.7.kg), custom_call_target="tpu_custom_call" | custom-call | tf_op jit(solution)/shard_map/copy_out/pallas_call | solution.py:480
